TPU v7x, 32 devices: a whole 2x2x4 slice. The times are simulated.
32 devices in a mesh: groups: 2 (over x), dom: 16 (over z, y, core).
Axes of the slice: x: 2, y: 2, z: 4, core: 2. Of those that a mesh axis runs over, the one named last changes fastest.
Arguments:
- fine_latent: bfloat16 [32768, 256], P(('groups', 'dom')), parts along dimension 0, may hold values from -6 to 6
- pool_owner: int32 [32768, 1], P(('groups', 'dom')), parts along dimension 0, may hold values from 0 to 15, as said below
- pool_local: int32 [32768], P(('groups', 'dom')), parts along dimension 0, may hold values from 0 to 63
- edge_latent: bfloat16 [8192, 256], P(('groups', 'dom')), parts along dimension 0, may hold values from -6 to 6
- src_owner: int32 [8192, 1], P(('groups', 'dom')), parts along dimension 0, may hold values from 0 to 15, as said below
- src_local: int32 [8192], P(('groups', 'dom')), parts along dimension 0, may hold values from 0 to 63
- dst_local: int32 [8192], P(('groups', 'dom')), parts along dimension 0, may hold values from 0 to 63
- edge_w1: bfloat16 [2, 768, 256], replicated, may hold values from -0.21875 to 0.21875
- edge_w2: bfloat16 [2, 256, 256], replicated, may hold values from -0.375 to 0.375
- node_w1: bfloat16 [2, 512, 256], replicated, may hold values from -0.25 to 0.25
- node_w2: bfloat16 [2, 256, 256], replicated, may hold values from -0.375 to 0.375
Outputs:
- fine_out: bfloat16 [32768, 256], P(('groups', 'dom')), parts along dimension 0
There are 2 independent parts, one for each index of `groups`. A program takes and returns all parts, laid end to end along the dimension named above; an argument that names none is the same for every part. Nothing has to cross between parts.
Inputs may be any that keep to these rules, and one draw needn't show every extreme that they name: `pool_owner`: each fine node of device d names d or one of the devices d - 2, d - 1, d + 1, d + 16 / 2 along dom (indices wrap around). Among the fine nodes of one device at most 64 name any one other device, and in every draw the nodes of some device name another device exactly 64 times. `src_owner`: each coarse edge of device d names d or one of the devices d - 2, d - 1, d + 1, d + 16 / 2 along dom (indices wrap around). Among the coarse edges of one device at most 16 name any one other device, and in every draw the edges of some device name another device exactly 16 times.
All inputs are finite; a program needn't handle non-finite values.
Results may differ from a plain program's by a relative error of at most 0.0095.
Values may be sent and summed in bfloat16 or wider, within the bound.
A program may use at most 64 MiB of HBM per device.

v0:
```python
import math

import jax
import jax.numpy as jnp
from jax import lax
from jax.sharding import PartitionSpec as P

LAYERS = 2


def layer_norm(values):
    center = values - jnp.mean(values, axis=-1, keepdims=True)
    spread = jnp.mean(center * center, axis=-1, keepdims=True)
    return center * lax.rsqrt(spread + 1e-05)


def make_picker(wanted, running, piece):
    piece_rows = piece.shape[0]
    block_rows = math.gcd(piece_rows, 1024)

    def make_one_block(block_index, inner):
        offset = block_index * block_rows
        chosen = lax.dynamic_slice_in_dim(piece, offset, block_rows, 0)
        onehot = (
            wanted[:, None] - offset == jnp.arange(block_rows, dtype=jnp.int32)[None, :]
        ).astype(jnp.bfloat16)
        return inner + jnp.dot(onehot, chosen, preferred_element_type=jnp.float32)

    return lax.fori_loop(0, piece_rows // block_rows, make_one_block, running)


def per_device(
    fine_latent,
    pool_owner,
    pool_local,
    edge_latent,
    src_owner,
    src_local,
    dst_local,
    edge_w1,
    edge_w2,
    node_w1,
    node_w2,
):
    fine_rows, feature_width = fine_latent.shape
    coarse_rows = fine_rows // 16
    edge_rows = edge_latent.shape[0]
    pool_target = pool_owner[:, 0]
    coarse_index = pool_target * coarse_rows + pool_local
    block_rows = math.gcd(coarse_rows * lax.axis_size("dom"), 1024)

    def pool_one_block(block_index):
        offset = block_index * block_rows
        onehot = (
            coarse_index[None, :] - offset == jnp.arange(block_rows, dtype=jnp.int32)[:, None]
        ).astype(jnp.bfloat16)
        return jnp.dot(onehot, fine_latent, preferred_element_type=jnp.float32)

    blocks = lax.map(
        pool_one_block,
        jnp.arange(coarse_rows * lax.axis_size("dom") // block_rows, dtype=jnp.int32),
    )
    pooled = lax.psum_scatter(
        blocks.reshape(coarse_rows * lax.axis_size("dom"), feature_width),
        "dom",
        scatter_dimension=0,
        tiled=True,
    )
    coarse = (pooled * 0.25).astype(jnp.bfloat16)
    edge_target = src_owner[:, 0]
    sender_index = edge_target * coarse_rows + src_local
    gather_onehot = (
        dst_local[None, :] == jnp.arange(coarse_rows, dtype=jnp.int32)[:, None]
    ).astype(jnp.bfloat16)
    edge_state = edge_latent
    for layer_index in range(LAYERS):
        empty = jnp.zeros((edge_rows, feature_width), jnp.float32)
        sender = make_picker(
            sender_index, empty, lax.all_gather(coarse, "dom", axis=0, tiled=True)
        ).astype(jnp.bfloat16)
        receiver = jnp.take(coarse, dst_local, axis=0)
        first_edge = edge_w1[layer_index]
        mixed = jnp.dot(sender, first_edge[:feature_width], preferred_element_type=jnp.float32)
        mixed = mixed + jnp.dot(
            receiver,
            first_edge[feature_width : 2 * feature_width],
            preferred_element_type=jnp.float32,
        )
        mixed = mixed + jnp.dot(
            edge_state, first_edge[2 * feature_width :], preferred_element_type=jnp.float32
        )
        hidden = jax.nn.relu(mixed).astype(jnp.bfloat16)
        update = layer_norm(
            jnp.dot(hidden, edge_w2[layer_index], preferred_element_type=jnp.float32)
        )
        edge_state = (edge_state.astype(jnp.float32) + update).astype(jnp.bfloat16)
        summed = jnp.dot(gather_onehot, edge_state, preferred_element_type=jnp.float32).astype(
            jnp.bfloat16
        )
        first_node = node_w1[layer_index]
        mixed = jnp.dot(coarse, first_node[:feature_width], preferred_element_type=jnp.float32)
        mixed = mixed + jnp.dot(
            summed, first_node[feature_width:], preferred_element_type=jnp.float32
        )
        hidden = jax.nn.relu(mixed).astype(jnp.bfloat16)
        update = layer_norm(
            jnp.dot(hidden, node_w2[layer_index], preferred_element_type=jnp.float32)
        )
        coarse = (coarse.astype(jnp.float32) + update).astype(jnp.bfloat16)
    empty_fine = jnp.zeros((fine_rows, feature_width), jnp.float32)
    lifted = make_picker(
        coarse_index, empty_fine, lax.all_gather(coarse, "dom", axis=0, tiled=True)
    )
    return (fine_latent.astype(jnp.float32) + lifted).astype(jnp.bfloat16)


def solution(mesh):
    placed = (
        P(("groups", "dom"), None),
        P(("groups", "dom"), None),
        P(("groups", "dom")),
        P(("groups", "dom"), None),
        P(("groups", "dom"), None),
        P(("groups", "dom")),
        P(("groups", "dom")),
        P(),
        P(),
        P(),
        P(),
    )
    return jax.shard_map(
        per_device,
        mesh=mesh,
        in_specs=placed,
        out_specs=P(("groups", "dom"), None),
        check_vma=False,
    )
```

profile of v0, /device:TPU:0, one launch (start us, length us, event | category | flops | bytes accessed | tf_op | source)
XLA Modules:
  0.0 147.9 jit_solution(14103513898065555512)
XLA Ops:
  6.5 0.0 reduce-scatter.2.cloned.1.call-start
  6.5 0.7 broadcast_multiply_fusion
  7.2 0.7 add.105
  7.9 2.8 %fusion.1 = f32[1024,256]{1,0:T(8,128)} fusion(bf16[1024,256]{1,0:T(8,128)(2,1)} %param.13, s32[1024]{0:T(1024)S(1)} %add.105), kind=kOutput, calls=%fused_computation.5 | convolution fusion | flops 537919488 | bytes 1576960 | tf_op jit(solution)/shard_map/while/body/eval_jaxpr/dot_general | solution.py:57
  10.7 0.0 copy-start.1
  10.7 0.0 copy-start.8
  10.7 0.0 copy-start.7
  10.7 0.0 copy-start.6
  10.8 0.0 reduce-scatter.2.cloned.1.call-update
  10.8 0.9 copy-done.1
  11.6 0.0 copy-start.2
  11.6 0.1 copy.12
  11.8 0.0 copy-done.8
  11.8 0.0 copy-done.7
  11.8 0.0 copy-done.6
  11.8 59.3 %reduce-scatter.2.cloned.1.call-done = f32[64,256]{1,0:T(8,128)} async-done(((f32[1024,256]{1,0:T(8,128)}), f32[64,256]{1,0:T(8,128)}) %reduce-scatter.2.cloned.1.call-update) | async-done | bytes 65552 | tf_op jit(solution)/shard_map/reduce_scatter | solution.py:63
  71.1 0.8 multiply_convert_fusion
  72.0 20.8 %all_gather.9 = bf16[1024,256]{1,0:T(8,128)(2,1)S(1)} all-gather(bf16[64,256]{1,0:T(8,128)(2,1)S(1)} %multiply_convert_fusion), channel_id=1, replica_groups=mesh['groups'=2,'dom'=16] {'dom'}, dimensions={0}, use_global_device_ids=true | all-gather | bytes 557056 | tf_op jit(solution)/shard_map/all_gather | solution.py:79
  92.8 1.1 gather_fusion
  93.9 0.0 copy-done.2
  93.9 0.0 copy-start.5
  93.9 0.5 fusion.10
  94.4 0.0 copy-start
  94.5 0.2 convolution_add_fusion.3
  94.7 0.2 copy-done.5
  94.9 0.0 copy-start.3
  94.9 0.4 fusion.78
  95.3 0.0 copy-start.4
  95.3 0.1 multiply_reduce_fusion.1
  95.4 0.1 copy-done
  95.5 0.1 fusion.40
  95.7 0.1 add_convert_fusion.1
  95.7 0.3 fusion.16
  96.0 0.0 copy-done.3
  96.0 0.2 fusion.81
  96.3 0.2 multiply_reduce_fusion.3
  96.5 0.0 copy-done.4
  96.5 0.1 add_convert_fusion.5
  96.6 18.9 %all_gather.10 = bf16[1024,256]{1,0:T(8,128)(2,1)S(1)} all-gather(bf16[64,256]{1,0:T(8,128)(2,1)S(1)} %add_convert_fusion.5), channel_id=1, replica_groups=mesh['groups'=2,'dom'=16] {'dom'}, dimensions={0}, use_global_device_ids=true | all-gather | bytes 557056 | tf_op jit(solution)/shard_map/all_gather | solution.py:79
  115.5 1.1 gather_fusion.1
  116.6 0.1 fusion.30
  116.8 0.5 fusion.11
  117.3 0.2 convolution_add_fusion.1
  117.5 0.4 fusion.82
  118.0 0.0 copy-start.9
  118.0 0.1 multiply_reduce_fusion
  118.1 0.3 fusion.17
  118.4 0.2 fusion.85
  118.7 0.2 multiply_reduce_fusion.2
  118.9 0.1 add_convert_fusion.4
  119.0 20.3 %all_gather.11 = bf16[1024,256]{1,0:T(8,128)(2,1)S(1)} all-gather(bf16[64,256]{1,0:T(8,128)(2,1)S(1)} %add_convert_fusion.4), channel_id=1, replica_groups=mesh['groups'=2,'dom'=16] {'dom'}, dimensions={0}, use_global_device_ids=true | all-gather | bytes 557056 | tf_op jit(solution)/shard_map/all_gather | solution.py:112
  139.3 0.0 copy-done.9
  139.3 1.7 %fusion.5 = bf16[1024,256]{1,0:T(8,128)(2,1)} fusion(bf16[1024,256]{1,0:T(8,128)(2,1)S(1)} %all_gather.11, s32[1024]{0:T(1024)S(1)} %add.105, bf16[1024,256]{1,0:T(8,128)(2,1)S(1)} %copy-done.9), kind=kOutput, calls=%fused_computation.9 | convolution fusion | flops 538705920 | bytes 1576960 | tf_op jit(solution)/shard_map/while/body/eval_jaxpr/dot_general | solution.py:27
  (13 shorter events, 0.1 us)
Async XLA Ops:
  6.5 64.6 %reduce-scatter.2.cloned.1.call-start = ((), (), s32[]{:S(2)}) async-start(), calls=%async_computation.1 | async-start | bytes 1114112 | tf_op jit(solution)/shard_map/reduce_scatter | solution.py:63
  10.7 0.9 copy-start.1
  10.7 1.0 copy-start.8
  10.7 1.0 copy-start.7
  10.7 1.1 copy-start.6
  11.6 82.3 %copy-start.2 = (bf16[2,768,256]{2,1,0:T(8,128)(2,1)S(1)}, bf16[2,768,256]{2,1,0:T(8,128)(2,1)}, u32[]{:S(2)}) copy-start(bf16[2,768,256]{2,1,0:T(8,128)(2,1)} %param.20) | copy-start | bytes 2359300
  93.9 1.0 copy-start.5
  94.4 1.1 copy-start
  94.9 1.1 copy-start.3
  95.3 1.2 copy-start.4
  118.0 21.3 %copy-start.9 = (bf16[1024,256]{1,0:T(8,128)(2,1)S(1)}, bf16[1024,256]{1,0:T(8,128)(2,1)}, u32[]{:S(2)}) copy-start(bf16[1024,256]{1,0:T(8,128)(2,1)} %param.13) | copy-start | bytes 1572868
Sparse Core Ops, SparseCore 0:
  11.0 60.1 reduce-scatter.1
where the time goes:
time: 148 us
  blocking collectives  60 us (41%)
  waiting for transfers between devices  59.3 us (40%)
  between operations  13.7 us (9%)
  matrix products  8.25 us (6%)
  local copies, waits for them, and re-layouts  3.62 us (2%)
  other arithmetic  3.01 us (2%)
    all_gather x3, blocking collectives, per_device(): lax.all_gather(coarse, 'dom', axis=0, tiled=True)  60 us
    reduce_scatter x1, waiting for transfers between devices, per_device(): lax.psum_scatter(blocks.reshape(coarse_rows * lax.axis_size('dom'), featu...  59.3 us
  transfers between devices with their start and end apart: 1, of which 1 were waited for; matrix products, arithmetic and copies ran while one was open for 0% of the time, Pallas kernels for 0%

commit v1 on v0

v1 whole, which is shorter than its diff:
```python
import functools

import jax
import jax.numpy as jnp
from jax import lax
from jax.experimental import pallas as pl
from jax.experimental.pallas import tpu as pltpu
from jax.sharding import PartitionSpec as P

LAYERS = 2
FINE_PER_COARSE = 16
CAP = 16
PARTNERS = 4
FAR = 3
CHUNKS = 4
ORDER = (3, 0, 1, 2)


def dot(a, b):
    return jnp.dot(a, b, preferred_element_type=jnp.float32)


def layer_norm(values):
    center = values - jnp.mean(values, axis=-1, keepdims=True)
    spread = jnp.mean(center * center, axis=-1, keepdims=True)
    return center * lax.rsqrt(spread + 1e-05)


def iota(shape, dim):
    return lax.broadcasted_iota(jnp.int32, shape, dim).astype(jnp.float32)


def onehot(a, b):
    return jnp.where(a == b, 1.0, 0.0).astype(jnp.bfloat16)


def to_column(row):
    wide = jnp.broadcast_to(row, (8, row.shape[1]))
    return jnp.transpose(wide)[:, 0:1]


def kernel(
    n,
    fine_hbm,
    pool_owner,
    pool_local,
    edge_hbm,
    src_owner,
    src_local,
    dst_local,
    ew1_hbm,
    ew2_hbm,
    nw1_hbm,
    nw2_hbm,
    out_hbm,
    fine,
    edges,
    ew1,
    ew2,
    nw1,
    nw2,
    lift_base,
    out,
    pool_send,
    pool_recv,
    want_send,
    want_recv,
    rows_send,
    rows_recv,
    last_send,
    last_recv,
    load_sem,
    store_sem,
    send_sem,
    recv_sem,
):
    fine_rows, width = fine.shape
    cn = fine_rows // FINE_PER_COARSE
    edge_rows = edges.shape[0]
    me = lax.axis_index("dom")
    offsets = (n - 2, n - 1, 1, n // 2)

    def ahead(k):
        return lax.rem(me + offsets[k], n)

    def behind(k):
        return lax.rem(me + n - offsets[k], n)

    barrier = pltpu.get_barrier_semaphore()
    for step in (1, 2, n // 2, n - 2, n - 1):
        pl.semaphore_signal(
            barrier,
            inc=1,
            device_id={"dom": lax.rem(me + step, n)},
            device_id_type=pl.DeviceIdType.MESH,
        )

    step_rows = fine_rows // CHUNKS
    loads = []
    for c in range(CHUNKS):
        part = pl.ds(c * step_rows, step_rows)
        loads.append((fine_hbm.at[part], fine.at[part]))
    loads += [
        (edge_hbm, edges),
        (ew1_hbm, ew1),
        (ew2_hbm, ew2),
        (nw1_hbm, nw1),
        (nw2_hbm, nw2),
    ]
    loads = [
        pltpu.make_async_copy(src, dst, load_sem.at[i]) for i, (src, dst) in enumerate(loads)
    ]
    for copy in loads:
        copy.start()

    def remote(stage, k, src, dst, target):
        return pltpu.make_async_remote_copy(
            src_ref=src,
            dst_ref=dst,
            send_sem=send_sem.at[stage, k],
            recv_sem=recv_sem.at[stage, k],
            device_id={"dom": target},
            device_id_type=pl.DeviceIdType.MESH,
        )

    def slot(owner):
        rel = owner - me
        rel = jnp.where(rel < 0, rel + n, rel)
        k = jnp.where(rel == 0, PARTNERS, FAR)
        for j in range(FAR):
            k = jnp.where(rel == offsets[j], j, k)
        return k

    pool_row = (slot(pool_owner[...]) * cn + pool_local[...]).astype(jnp.float32)
    total = jnp.zeros((PARTNERS * cn, width), jnp.float32)
    own = jnp.zeros((cn, width), jnp.float32)
    for c in range(CHUNKS):
        piece = pool_row[:, c * step_rows : (c + 1) * step_rows]
        away = onehot(piece, iota((PARTNERS * cn, step_rows), 0))
        loads[c].wait()
        total += dot(away, fine[pl.ds(c * step_rows, step_rows), :])
    pool_send[...] = total.astype(jnp.bfloat16)
    pl.semaphore_wait(barrier, 5)
    sends = []
    pool_copies = [
        remote(0, k, pool_send.at[pl.ds(k * cn, cn)], pool_recv.at[pl.ds(k * cn, cn)], ahead(k))
        for k in range(PARTNERS)
    ]
    for k in ORDER:
        pool_copies[k].start()
    sends += pool_copies

    src_slot = slot(src_owner[...])
    src_row = src_local[...].astype(jnp.float32)
    dst_row = dst_local[...].astype(jnp.float32)
    slot_row = src_slot.astype(jnp.float32)
    by_slot = onehot(slot_row, iota((8, edge_rows), 0))
    earlier = jnp.where(
        iota((edge_rows, edge_rows), 0) < iota((edge_rows, edge_rows), 1), 1.0, 0.0
    ).astype(jnp.bfloat16)
    ranks = dot(by_slot, earlier)
    rank = jnp.sum(ranks * by_slot.astype(jnp.float32), axis=0, keepdims=True)
    away_row = jnp.where(src_slot < PARTNERS, slot_row * CAP + rank, -1.0)
    own_src_row = jnp.where(src_slot < PARTNERS, -1.0, src_row)
    src_col = to_column(src_row)
    want = dot(
        onehot(away_row, iota((PARTNERS * CAP, edge_rows), 0)),
        onehot(src_col, iota((edge_rows, want_send.shape[1]), 1)),
    )
    want_send[...] = want.astype(jnp.bfloat16)
    want_copies = [
        remote(
            1, k, want_send.at[pl.ds(k * CAP, CAP)], want_recv.at[pl.ds(k * CAP, CAP)], ahead(k)
        )
        for k in range(PARTNERS)
    ]
    for k in ORDER:
        want_copies[k].start()
    sends += want_copies

    for c in range(CHUNKS):
        piece = pool_row[:, c * step_rows : (c + 1) * step_rows] - PARTNERS * cn
        own += dot(
            onehot(piece, iota((cn, step_rows), 0)), fine[pl.ds(c * step_rows, step_rows), :]
        )
    take_away = onehot(to_column(away_row), iota((edge_rows, PARTNERS * CAP), 1))
    take_own = onehot(to_column(own_src_row), iota((edge_rows, cn), 1))
    take_dst = onehot(to_column(dst_row), iota((edge_rows, cn), 1))
    add_dst = onehot(dst_row, iota((cn, edge_rows), 0))
    pool_col = to_column(pool_row)
    for copy in loads[CHUNKS:]:
        copy.wait()
    edge_state = edges[...]

    for copy in pool_copies:
        copy.wait_recv()
    for k in range(PARTNERS):
        own += pool_recv[pl.ds(k * cn, cn), :].astype(jnp.float32)
    coarse = (own * 0.25).astype(jnp.bfloat16)
    for copy in want_copies:
        copy.wait_recv()

    for layer in range(LAYERS):
        rows_send[layer] = dot(want_recv[:, :cn], coarse).astype(jnp.bfloat16)
        row_copies = [
            remote(
                2 + layer,
                k,
                rows_send.at[layer, pl.ds(k * CAP, CAP)],
                rows_recv.at[layer, pl.ds(k * CAP, CAP)],
                behind(k),
            )
            for k in range(PARTNERS)
        ]
        for k in ORDER:
            row_copies[k].start()
        sends += row_copies
        mixed = dot(edge_state, ew1[layer, 2 * width :, :])
        mixed += dot(dot(take_own, coarse).astype(jnp.bfloat16), ew1[layer, :width, :])
        mixed += dot(dot(take_dst, coarse).astype(jnp.bfloat16), ew1[layer, width : 2 * width, :])
        node_mixed = dot(coarse, nw1[layer, :width, :])
        for copy in row_copies:
            copy.wait_recv()
        sender = dot(take_away, rows_recv[layer]).astype(jnp.bfloat16)
        mixed += dot(sender, ew1[layer, :width, :])
        hidden = jnp.maximum(mixed, 0.0).astype(jnp.bfloat16)
        update = layer_norm(dot(hidden, ew2[layer]))
        edge_state = (edge_state.astype(jnp.float32) + update).astype(jnp.bfloat16)
        summed = dot(add_dst, edge_state).astype(jnp.bfloat16)
        node_mixed += dot(summed, nw1[layer, width:, :])
        hidden = jnp.maximum(node_mixed, 0.0).astype(jnp.bfloat16)
        update = layer_norm(dot(hidden, nw2[layer]))
        coarse = (coarse.astype(jnp.float32) + update).astype(jnp.bfloat16)

    last_send[...] = coarse
    last_copies = [
        remote(2 + LAYERS, k, last_send, last_recv.at[pl.ds(k * cn, cn)], behind(k))
        for k in range(PARTNERS)
    ]
    for k in ORDER:
        last_copies[k].start()
    sends += last_copies
    take_base = onehot(pool_col - PARTNERS * cn, iota((fine_rows, cn), 1))
    lift_base[...] = fine[...].astype(jnp.float32) + dot(take_base, coarse)
    take_far = onehot(pool_col, iota((fine_rows, PARTNERS * cn), 1))
    for copy in last_copies:
        copy.wait_recv()
    stores = []
    for c in range(CHUNKS):
        part = pl.ds(c * step_rows, step_rows)
        lifted = dot(take_far[c * step_rows : (c + 1) * step_rows], last_recv[...])
        out[part, :] = (lift_base[part, :] + lifted).astype(jnp.bfloat16)
        copy = pltpu.make_async_copy(out.at[part], out_hbm.at[part], store_sem.at[c])
        copy.start()
        stores.append(copy)
    for copy in sends:
        copy.wait_send()
    for copy in stores:
        copy.wait()


def per_device(
    n,
    fine_latent,
    pool_owner,
    pool_local,
    edge_latent,
    src_owner,
    src_local,
    dst_local,
    edge_w1,
    edge_w2,
    node_w1,
    node_w2,
):
    fine_rows, width = fine_latent.shape
    edge_rows = edge_latent.shape[0]
    cn = fine_rows // FINE_PER_COARSE
    lanes = -(-cn // 128) * 128
    hbm = pl.BlockSpec(memory_space=pl.ANY)
    vmem = pl.BlockSpec(memory_space=pltpu.VMEM)
    bf16 = jnp.bfloat16
    stages = 3 + LAYERS
    return pl.pallas_call(
        functools.partial(kernel, n),
        out_shape=jax.ShapeDtypeStruct((fine_rows, width), bf16),
        in_specs=[hbm, vmem, vmem, hbm, vmem, vmem, vmem, hbm, hbm, hbm, hbm],
        out_specs=hbm,
        scratch_shapes=[
            pltpu.VMEM((fine_rows, width), bf16),
            pltpu.VMEM((edge_rows, width), bf16),
            pltpu.VMEM(edge_w1.shape, bf16),
            pltpu.VMEM(edge_w2.shape, bf16),
            pltpu.VMEM(node_w1.shape, bf16),
            pltpu.VMEM(node_w2.shape, bf16),
            pltpu.VMEM((fine_rows, width), jnp.float32),
            pltpu.VMEM((fine_rows, width), bf16),
            pltpu.VMEM((PARTNERS * cn, width), bf16),
            pltpu.VMEM((PARTNERS * cn, width), bf16),
            pltpu.VMEM((PARTNERS * CAP, lanes), bf16),
            pltpu.VMEM((PARTNERS * CAP, lanes), bf16),
            pltpu.VMEM((LAYERS, PARTNERS * CAP, width), bf16),
            pltpu.VMEM((LAYERS, PARTNERS * CAP, width), bf16),
            pltpu.VMEM((cn, width), bf16),
            pltpu.VMEM((PARTNERS * cn, width), bf16),
            pltpu.SemaphoreType.DMA((CHUNKS + 5,)),
            pltpu.SemaphoreType.DMA((CHUNKS,)),
            pltpu.SemaphoreType.DMA((stages, PARTNERS)),
            pltpu.SemaphoreType.DMA((stages, PARTNERS)),
        ],
        compiler_params=pltpu.CompilerParams(
            collective_id=0, has_side_effects=True, vmem_limit_bytes=60 * 1024 * 1024
        ),
    )(
        fine_latent,
        pool_owner.reshape(1, fine_rows),
        pool_local.reshape(1, fine_rows),
        edge_latent,
        src_owner.reshape(1, edge_rows),
        src_local.reshape(1, edge_rows),
        dst_local.reshape(1, edge_rows),
        edge_w1,
        edge_w2,
        node_w1,
        node_w2,
    )


def solution(mesh):
    rows = P(("groups", "dom"), None)
    line = P(("groups", "dom"))
    return jax.shard_map(
        functools.partial(per_device, mesh.shape["dom"]),
        mesh=mesh,
        in_specs=(rows, rows, line, rows, rows, line, line, P(), P(), P(), P()),
        out_specs=rows,
        check_vma=False,
    )
```

time: 148 us -> 30.3 us (0.20)
  blocking collectives: 60 us -> 0 us
  waiting for transfers between devices: 59.3 us -> 0 us
  Pallas kernels: 0 us -> 28.2 us
  between operations: 13.7 us -> 0.01 us
  matrix products: 8.25 us -> 0 us
  other arithmetic: 3.01 us -> 0 us
  local copies, waits for them, and re-layouts: 3.62 us -> 1.87 us
    all_gather x3 -> x0, blocking collectives: 60 us -> none  [per_device(): lax.all_gather(coarse, 'dom', axis=0, tiled=True)]
    reduce_scatter x1 -> x0, waiting for transfers between devices: 59.3 us -> none  [per_device(): lax.psum_scatter(blocks.reshape(coarse_rows * lax.axis_size('dom'), featu...]
    pallas_call x0 -> x1, Pallas kernels: none -> 28.2 us  [per_device(): pl.pallas_call(functools.partial(kernel, n), out_shape=jax.ShapeDtypeStru...]
    dot_general x14 -> x0, matrix products: 8.25 us -> none  [the longest x1 2.82 us: pool_one_block(): return jnp.dot(onehot, fine_latent, preferred_element_type=jnp.float32)]
    gather x2 -> x0, local copies, waits for them, and re-layouts: 2.3 us -> none  [per_device(): receiver = jnp.take(coarse, dst_local, axis=0)]
  transfers between devices with their start and end apart: 1 -> 0, of which waited for: 1 -> 0; matrix products, arithmetic and copies ran while one was open for 0% -> 0% of each run, Pallas kernels for 0% -> 0%
where the time goes in v1:
time: 30.3 us; the launch traced here: 30.1 us
  Pallas kernels  28.2 us (93%)
  local copies, waits for them, and re-layouts  1.87 us (6%)
    pallas_call x1, Pallas kernels, per_device(): pl.pallas_call(functools.partial(kernel, n), out_shape=jax.ShapeDtypeStru...  28.2 us
    unnamed x1, local copies, waits for them, and re-layouts  1.87 us

profile of v1, /device:TPU:0, one launch (start us, length us, event | category | flops | bytes accessed | tf_op | source)
XLA Modules:
  0.0 30.1 jit_solution(11590006722963607861)
XLA Ops:
  0.0 28.2 %shard_map.109 = bf16[1024,256]{1,0:T(8,128)(2,1)} custom-call(bf16[1024,256]{1,0:T(8,128)(2,1)} %fine_hbm.1, s32[1,1024]{1,0:T(1,128)} %bitcast.5, s32[1,1024]{1,0:T(1,128)} %bitcast.6, bf16[256,256]{1,0:T(8,128)(2,1)} %edge_hbm.1, s32[1,256]{1,0:T(1,128)} %bitcast.7, s32[1,256]{1,0:T(1,128)} %bitcast.8, s32[1,256]{1,0:T(1,128)} %bitcast.9, ...), custom_call_target="tpu_custom_call" | custom-call | tf_op jit(solution)/shard_map/pallas_call | solution.py:284
  28.2 1.9 %copy.13 = bf16[1024,256]{1,0:T(8,128)(2,1)} copy(bf16[1024,256]{1,0:T(8,128)(2,1)} %shard_map.109) | data formatting | bytes 1048576

commit v2 on v1

--- a/solution.py
+++ b/solution.py
@@ -13,7 +13,7 @@
 PARTNERS = 4
 FAR = 3
 CHUNKS = 4
-ORDER = (3, 0, 1, 2)
+ORDER = (1, 2, 0, 3)
 
 
 def dot(a, b):
@@ -42,17 +42,22 @@
 def kernel(
     n,
     fine_hbm,
-    pool_owner,
-    pool_local,
+    pool_owner_hbm,
+    pool_local_hbm,
     edge_hbm,
-    src_owner,
-    src_local,
-    dst_local,
+    src_owner_hbm,
+    src_local_hbm,
+    dst_local_hbm,
     ew1_hbm,
     ew2_hbm,
     nw1_hbm,
     nw2_hbm,
-    out_hbm,
+    out,
+    pool_owner,
+    pool_local,
+    src_owner,
+    src_local,
+    dst_local,
     fine,
     edges,
     ew1,
@@ -60,7 +65,6 @@
     nw1,
     nw2,
     lift_base,
-    out,
     pool_send,
     pool_recv,
     want_send,
@@ -70,7 +74,6 @@
     last_send,
     last_recv,
     load_sem,
-    store_sem,
     send_sem,
     recv_sem,
 ):
@@ -87,7 +90,7 @@
         return lax.rem(me + n - offsets[k], n)
 
     barrier = pltpu.get_barrier_semaphore()
-    for step in (1, 2, n // 2, n - 2, n - 1):
+    for step in (1, n - 1, 2, n - 2, n // 2):
         pl.semaphore_signal(
             barrier,
             inc=1,
@@ -96,11 +99,14 @@
         )
 
     step_rows = fine_rows // CHUNKS
-    loads = []
+    loads = [(pool_owner_hbm, pool_owner), (pool_local_hbm, pool_local)]
     for c in range(CHUNKS):
         part = pl.ds(c * step_rows, step_rows)
         loads.append((fine_hbm.at[part], fine.at[part]))
     loads += [
+        (src_owner_hbm, src_owner),
+        (src_local_hbm, src_local),
+        (dst_local_hbm, dst_local),
         (edge_hbm, edges),
         (ew1_hbm, ew1),
         (ew2_hbm, ew2),
@@ -131,13 +137,18 @@
             k = jnp.where(rel == offsets[j], j, k)
         return k
 
+    def arrive(first, last):
+        for copy in loads[first:last]:
+            copy.wait()
+
+    arrive(0, 2)
     pool_row = (slot(pool_owner[...]) * cn + pool_local[...]).astype(jnp.float32)
     total = jnp.zeros((PARTNERS * cn, width), jnp.float32)
     own = jnp.zeros((cn, width), jnp.float32)
     for c in range(CHUNKS):
         piece = pool_row[:, c * step_rows : (c + 1) * step_rows]
         away = onehot(piece, iota((PARTNERS * cn, step_rows), 0))
-        loads[c].wait()
+        arrive(2 + c, 3 + c)
         total += dot(away, fine[pl.ds(c * step_rows, step_rows), :])
     pool_send[...] = total.astype(jnp.bfloat16)
     pl.semaphore_wait(barrier, 5)
@@ -150,6 +161,7 @@
         pool_copies[k].start()
     sends += pool_copies
 
+    arrive(2 + CHUNKS, 5 + CHUNKS)
     src_slot = slot(src_owner[...])
     src_row = src_local[...].astype(jnp.float32)
     dst_row = dst_local[...].astype(jnp.float32)
@@ -188,8 +200,7 @@
     take_dst = onehot(to_column(dst_row), iota((edge_rows, cn), 1))
     add_dst = onehot(dst_row, iota((cn, edge_rows), 0))
     pool_col = to_column(pool_row)
-    for copy in loads[CHUNKS:]:
-        copy.wait()
+    arrive(5 + CHUNKS, len(loads))
     edge_state = edges[...]
 
     for copy in pool_copies:
@@ -245,18 +256,12 @@
     take_far = onehot(pool_col, iota((fine_rows, PARTNERS * cn), 1))
     for copy in last_copies:
         copy.wait_recv()
-    stores = []
     for c in range(CHUNKS):
         part = pl.ds(c * step_rows, step_rows)
         lifted = dot(take_far[c * step_rows : (c + 1) * step_rows], last_recv[...])
         out[part, :] = (lift_base[part, :] + lifted).astype(jnp.bfloat16)
-        copy = pltpu.make_async_copy(out.at[part], out_hbm.at[part], store_sem.at[c])
-        copy.start()
-        stores.append(copy)
     for copy in sends:
         copy.wait_send()
-    for copy in stores:
-        copy.wait()
 
 
 def per_device(
@@ -277,16 +282,21 @@
     edge_rows = edge_latent.shape[0]
     cn = fine_rows // FINE_PER_COARSE
     lanes = -(-cn // 128) * 128
-    hbm = pl.BlockSpec(memory_space=pl.ANY)
+    hbm = pl.BlockSpec(memory_space=pltpu.HBM)
     vmem = pl.BlockSpec(memory_space=pltpu.VMEM)
     bf16 = jnp.bfloat16
     stages = 3 + LAYERS
     return pl.pallas_call(
         functools.partial(kernel, n),
-        out_shape=jax.ShapeDtypeStruct((fine_rows, width), bf16),
-        in_specs=[hbm, vmem, vmem, hbm, vmem, vmem, vmem, hbm, hbm, hbm, hbm],
-        out_specs=hbm,
+        out_shape=pltpu.VMEM((fine_rows, width), bf16),
+        in_specs=[hbm] * 11,
+        out_specs=vmem,
         scratch_shapes=[
+            pltpu.VMEM((1, fine_rows), jnp.int32),
+            pltpu.VMEM((1, fine_rows), jnp.int32),
+            pltpu.VMEM((1, edge_rows), jnp.int32),
+            pltpu.VMEM((1, edge_rows), jnp.int32),
+            pltpu.VMEM((1, edge_rows), jnp.int32),
             pltpu.VMEM((fine_rows, width), bf16),
             pltpu.VMEM((edge_rows, width), bf16),
             pltpu.VMEM(edge_w1.shape, bf16),
@@ -294,7 +304,6 @@
             pltpu.VMEM(node_w1.shape, bf16),
             pltpu.VMEM(node_w2.shape, bf16),
             pltpu.VMEM((fine_rows, width), jnp.float32),
-            pltpu.VMEM((fine_rows, width), bf16),
             pltpu.VMEM((PARTNERS * cn, width), bf16),
             pltpu.VMEM((PARTNERS * cn, width), bf16),
             pltpu.VMEM((PARTNERS * CAP, lanes), bf16),
@@ -303,8 +312,7 @@
             pltpu.VMEM((LAYERS, PARTNERS * CAP, width), bf16),
             pltpu.VMEM((cn, width), bf16),
             pltpu.VMEM((PARTNERS * cn, width), bf16),
-            pltpu.SemaphoreType.DMA((CHUNKS + 5,)),
-            pltpu.SemaphoreType.DMA((CHUNKS,)),
+            pltpu.SemaphoreType.DMA((CHUNKS + 10,)),
             pltpu.SemaphoreType.DMA((stages, PARTNERS)),
             pltpu.SemaphoreType.DMA((stages, PARTNERS)),
         ],

time: 30.3 us -> 27 us (0.89)
  Pallas kernels: 28.2 us -> 26 us
  local copies, waits for them, and re-layouts: 1.87 us -> 0.8 us
    pallas_call x1, Pallas kernels: 28.2 us -> 26 us  [per_device(): pl.pallas_call(functools.partial(kernel, n), out_shape=pltpu.VMEM((fine_r...]
    unnamed x1, local copies, waits for them, and re-layouts: 1.87 us -> 0.8 us
where the time goes in v2:
time: 27 us; the launch traced here: 26.8 us
  Pallas kernels  26 us (96%)
  local copies, waits for them, and re-layouts  0.8 us (3%)
    pallas_call x1, Pallas kernels, per_device(): pl.pallas_call(functools.partial(kernel, n), out_shape=pltpu.VMEM((fine_r...  26 us
    unnamed x1, local copies, waits for them, and re-layouts  0.8 us

profile of v2, /device:TPU:0, one launch (start us, length us, event | category | flops | bytes accessed | tf_op | source)
XLA Modules:
  0.0 26.8 jit_solution(12614995833518628474)
XLA Ops:
  0.0 26.0 %shard_map.109 = bf16[1024,256]{1,0:T(8,128)(2,1)S(1)} custom-call(bf16[1024,256]{1,0:T(8,128)(2,1)} %fine_hbm.1, s32[1,1024]{1,0:T(1,128)} %bitcast.5, s32[1,1024]{1,0:T(1,128)} %bitcast.6, bf16[256,256]{1,0:T(8,128)(2,1)} %edge_hbm.1, s32[1,256]{1,0:T(1,128)} %bitcast.7, s32[1,256]{1,0:T(1,128)} %bitcast.8, s32[1,256]{1,0:T(1,128)} %bitcast.9, ...), custom_call_target="tpu_custom_call" | custom-call | tf_op jit(solution)/shard_map/pallas_call | solution.py:289
  26.0 0.8 %copy.13 = bf16[1024,256]{1,0:T(8,128)(2,1)} copy(bf16[1024,256]{1,0:T(8,128)(2,1)S(1)} %shard_map.109) | data formatting | bytes 1048576

commit v3 on v2

--- a/solution.py
+++ b/solution.py
@@ -52,7 +52,9 @@
     ew2_hbm,
     nw1_hbm,
     nw2_hbm,
-    out,
+    lift_base,
+    take_far,
+    lift_rows,
     pool_owner,
     pool_local,
     src_owner,
@@ -64,7 +66,6 @@
     ew2,
     nw1,
     nw2,
-    lift_base,
     pool_send,
     pool_recv,
     want_send,
@@ -157,7 +158,7 @@
         remote(0, k, pool_send.at[pl.ds(k * cn, cn)], pool_recv.at[pl.ds(k * cn, cn)], ahead(k))
         for k in range(PARTNERS)
     ]
-    for k in ORDER:
+    for k in (1, 0, 2, 3):
         pool_copies[k].start()
     sends += pool_copies
 
@@ -200,6 +201,7 @@
     take_dst = onehot(to_column(dst_row), iota((edge_rows, cn), 1))
     add_dst = onehot(dst_row, iota((cn, edge_rows), 0))
     pool_col = to_column(pool_row)
+    take_far[...] = onehot(pool_col, iota((fine_rows, PARTNERS * cn), 1))
     arrive(5 + CHUNKS, len(loads))
     edge_state = edges[...]
 
@@ -253,15 +255,24 @@
     sends += last_copies
     take_base = onehot(pool_col - PARTNERS * cn, iota((fine_rows, cn), 1))
     lift_base[...] = fine[...].astype(jnp.float32) + dot(take_base, coarse)
-    take_far = onehot(pool_col, iota((fine_rows, PARTNERS * cn), 1))
     for copy in last_copies:
         copy.wait_recv()
+    lift_rows[...] = last_recv[...]
+    for copy in sends:
+        copy.wait_send()
+
+
+def lift_kernel(base, take, rows, out_hbm, out, store_sem):
+    step_rows = base.shape[0] // CHUNKS
+    stores = []
     for c in range(CHUNKS):
         part = pl.ds(c * step_rows, step_rows)
-        lifted = dot(take_far[c * step_rows : (c + 1) * step_rows], last_recv[...])
-        out[part, :] = (lift_base[part, :] + lifted).astype(jnp.bfloat16)
-    for copy in sends:
-        copy.wait_send()
+        out[part, :] = (base[part, :] + dot(take[part, :], rows[...])).astype(jnp.bfloat16)
+        copy = pltpu.make_async_copy(out.at[part], out_hbm.at[part], store_sem.at[c])
+        copy.start()
+        stores.append(copy)
+    for copy in stores:
+        copy.wait()
 
 
 def per_device(
@@ -286,11 +297,15 @@
     vmem = pl.BlockSpec(memory_space=pltpu.VMEM)
     bf16 = jnp.bfloat16
     stages = 3 + LAYERS
-    return pl.pallas_call(
+    base, take, rows = pl.pallas_call(
         functools.partial(kernel, n),
-        out_shape=pltpu.VMEM((fine_rows, width), bf16),
+        out_shape=(
+            pltpu.VMEM((fine_rows, width), jnp.float32),
+            pltpu.VMEM((fine_rows, PARTNERS * cn), bf16),
+            pltpu.VMEM((PARTNERS * cn, width), bf16),
+        ),
         in_specs=[hbm] * 11,
-        out_specs=vmem,
+        out_specs=(vmem, vmem, vmem),
         scratch_shapes=[
             pltpu.VMEM((1, fine_rows), jnp.int32),
             pltpu.VMEM((1, fine_rows), jnp.int32),
@@ -303,7 +318,6 @@
             pltpu.VMEM(edge_w2.shape, bf16),
             pltpu.VMEM(node_w1.shape, bf16),
             pltpu.VMEM(node_w2.shape, bf16),
-            pltpu.VMEM((fine_rows, width), jnp.float32),
             pltpu.VMEM((PARTNERS * cn, width), bf16),
             pltpu.VMEM((PARTNERS * cn, width), bf16),
             pltpu.VMEM((PARTNERS * CAP, lanes), bf16),
@@ -332,6 +346,17 @@
         node_w1,
         node_w2,
     )
+    return pl.pallas_call(
+        lift_kernel,
+        out_shape=jax.ShapeDtypeStruct((fine_rows, width), bf16),
+        in_specs=[vmem, vmem, vmem],
+        out_specs=hbm,
+        scratch_shapes=[
+            pltpu.VMEM((fine_rows, width), bf16),
+            pltpu.SemaphoreType.DMA((CHUNKS,)),
+        ],
+        compiler_params=pltpu.CompilerParams(vmem_limit_bytes=16 * 1024 * 1024),
+    )(base, take, rows)
 
 
 def solution(mesh):

time: 27 us -> 26.8 us (level)
  local copies, waits for them, and re-layouts: 0.8 us -> 0 us
  Pallas kernels: 26 us -> 26.7 us
    unnamed x1 -> x0, local copies, waits for them, and re-layouts: 0.8 us -> none
    pallas_call x1 -> x2, Pallas kernels: 26 us -> 26.7 us  [the longest x1 25.6 us: per_device(): pl.pallas_call(functools.partial(kernel, n), out_shape=(pltpu.VMEM((fine_...]
where the time goes in v3:
time: 26.8 us; the launch traced here: 26.7 us
  Pallas kernels  26.7 us (100%)
    pallas_call x1, Pallas kernels, per_device(): pl.pallas_call(functools.partial(kernel, n), out_shape=(pltpu.VMEM((fine_...  25.6 us
    pallas_call x1, Pallas kernels, per_device(): pl.pallas_call(lift_kernel, out_shape=jax.ShapeDtypeStruct((fine_rows, wi...  1.05 us

profile of v3, /device:TPU:0, one launch (start us, length us, event | category | flops | bytes accessed | tf_op | source)
XLA Modules:
  0.0 26.7 jit_solution(9536157771887592068)
XLA Ops:
  0.0 25.6 %shard_map.109 = (f32[1024,256]{1,0:T(8,128)S(1)}, bf16[1024,256]{1,0:T(8,128)(2,1)S(1)}, bf16[256,256]{1,0:T(8,128)(2,1)S(1)}) custom-call(bf16[1024,256]{1,0:T(8,128)(2,1)} %fine_hbm.1, s32[1,1024]{1,0:T(1,128)} %bitcast.5, s32[1,1024]{1,0:T(1,128)} %bitcast.6, bf16[256,256]{1,0:T(8,128)(2,1)} %edge_hbm.1, s32[1,256]{1,0:T(1,128)} %bitcast.7, ...), custom_call_target="tpu_custom_call" | custom-call | tf_op jit(solution)/shard_map/pallas_call | solution.py:300
  25.6 1.1 %shard_map.110 = bf16[1024,256]{1,0:T(8,128)(2,1)} custom-call(f32[1024,256]{1,0:T(8,128)S(1)} %get-tuple-element.8.base, bf16[1024,256]{1,0:T(8,128)(2,1)S(1)} %get-tuple-element.9.take, bf16[256,256]{1,0:T(8,128)(2,1)S(1)} %get-tuple-element.10.rows), custom_call_target="tpu_custom_call" | custom-call | tf_op jit(solution)/shard_map/pallas_call | solution.py:349
